TPU v7x, 256 devices: a whole 4x4x8 slice. The times are simulated.
256 devices in a mesh: dp: 64 (over y, z, core), seq: 4 (over x).
Axes of the slice: x: 4, y: 4, z: 8, core: 2. Of those that a mesh axis runs over, the one named last changes fastest.
Arguments:
- layer_in: bfloat16 [64, 1024, 4096], P('dp', 'seq'), may hold values from -6 to 6
- head_in: bfloat16 [64, 1024, 4096], P('dp', 'seq'), may hold values from -6 to 6
- ids: int32 [64, 1024], P('dp', 'seq'), may hold values from 0 to 5, never falling along the last dimension, each value on 1 to 512 neighbouring positions
- dy: bfloat16 [64, 1024, 4096], P('dp', 'seq'), may hold values from -6 to 6
- w_in: bfloat16 [4096, 320], P('dp'), may hold values from -0.09375 to 0.09375
- a_log: float32 [64], replicated, may hold values from -3 to 0.7
- dt_bias: float32 [64], replicated, may hold values from -5 to -3
- d_skip: float32 [64], replicated, may hold values from 0.5 to 1.5
Outputs:
- layer_out: bfloat16 [64, 1024, 4096], P('dp', 'seq')
- grad_x: bfloat16 [64, 1024, 4096], P('dp', 'seq')
- grad_u: bfloat16 [64, 1024, 4096], P('dp', 'seq')
- grad_w: float32 [4096, 320], P('dp')
Inputs may be any that keep to these rules, and one draw needn't show every extreme that they name: `ids`: document numbers never fall along a sequence; no document is longer than 512 positions.
All inputs are finite; a program needn't handle non-finite values.
Results may differ from a plain program's by a relative error of at most 0.0049.
Values may be sent and summed in bfloat16 or wider, within the bound.
No kernel may reach another device: no remote copies, remote signals or barrier semaphores. Data moves between devices by JAX's collectives and lax.ppermute only.
A program may use at most 128 MiB of HBM per device.

v0:
```python
import jax
import jax.numpy as jnp
from jax import lax
from jax.sharding import PartitionSpec as P


def passed_along(value, axis, steps):
    count = lax.axis_size(axis)
    leading, last = (max(0, -steps), min(count, count - steps))
    return lax.ppermute(value, axis, [(source, source + steps) for source in range(leading, last)])


def span_forward(proj, xf, ids, a_log, dt_bias, d_skip, h_in):
    length = proj.shape[0]
    heads = a_log.shape[0]
    state = (proj.shape[1] - heads) // 2
    b_mat = proj[:, :state]
    c_mat = proj[:, state : 2 * state]
    step = jax.nn.softplus(proj[:, 2 * state :] + dt_bias[None, :])
    cum = jnp.cumsum(-step * jnp.exp(a_log)[None, :], axis=0)
    order = jnp.arange(length)
    keep = (ids[:, None] == ids[None, :]) & (order[:, None] >= order[None, :])
    scores = jnp.dot(c_mat, b_mat.T, precision=lax.Precision.HIGHEST)
    gap = jnp.where(keep[None], cum.T[:, :, None] - cum.T[:, None, :], -1e30)
    mixing = jnp.exp(gap) * scores[None] * step.T[:, None, :]
    xh = xf.reshape(length, heads, -1)
    intra = jnp.einsum("hts,shp->thp", mixing, xh, precision=lax.Precision.HIGHEST)
    lead = (ids == ids[0]).astype(jnp.float32)
    reach = lead[:, None] * jnp.exp(cum)
    carried = jnp.einsum("tn,hpn->thp", c_mat, h_in, precision=lax.Precision.HIGHEST)
    out = intra + reach[:, :, None] * carried + d_skip[None, :, None] * xh
    tail = (ids == ids[-1]).astype(jnp.float32)
    end_w = tail[:, None] * jnp.exp(cum[-1][None, :] - cum) * step
    s_end = jnp.einsum(
        "thp,tn->hpn", xh * end_w[:, :, None], b_mat, precision=lax.Precision.HIGHEST
    )
    whole = (ids[0] == ids[-1]).astype(jnp.float32)
    h_out = s_end + (whole * jnp.exp(cum[-1]))[:, None, None] * h_in
    return (out.reshape(length, -1), h_out)


def span_ends(proj, xf, ids, a_log, dt_bias):
    length = proj.shape[0]
    heads = a_log.shape[0]
    state = (proj.shape[1] - heads) // 2
    b_mat = proj[:, :state]
    c_mat = proj[:, state : 2 * state]
    step = jax.nn.softplus(proj[:, 2 * state :] + dt_bias[None, :])
    cum = jnp.cumsum(-step * jnp.exp(a_log)[None, :], axis=0)
    xh = xf.reshape(length, heads, -1)
    tail = (ids == ids[-1]).astype(jnp.float32)
    end_w = tail[:, None] * jnp.exp(cum[-1][None, :] - cum) * step
    s_end = jnp.einsum(
        "thp,tn->hpn", xh * end_w[:, :, None], b_mat, precision=lax.Precision.HIGHEST
    )
    whole = (ids[0] == ids[-1]).astype(jnp.float32)
    lead = (ids == ids[0]).astype(jnp.float32)
    return (s_end, whole * jnp.exp(cum[-1]), c_mat, lead[:, None] * jnp.exp(cum))


def body(layer_in, head_in, ids, dy, w_in, a_log, dt_bias, d_skip):
    weights = lax.all_gather(w_in, "dp", axis=0, tiled=True)
    u_rows = layer_in[0]
    proj = jnp.dot(u_rows, weights, preferred_element_type=jnp.float32)
    xf = head_in[0].astype(jnp.float32)
    id_row = ids[0]
    heads = a_log.shape[0]
    length = id_row.shape[0]
    count = lax.axis_size("seq")
    first_id = (id_row[0] + 1).astype(jnp.float32)
    sent_id = jnp.reshape(id_row[-1] + 1, (1,)).astype(jnp.float32)
    s_end, a_end, c_mat, reach = span_ends(proj, xf, id_row, a_log, dt_bias)
    dyf = dy[0].astype(jnp.float32)
    scaled = dyf.reshape(length, heads, -1) * reach[:, :, None]
    grad_in = jnp.einsum("thp,tn->hpn", scaled, c_mat, precision=lax.Precision.HIGHEST)
    link = jnp.zeros((), jnp.float32)
    prefix = jnp.zeros_like(s_end)
    for turn in range(count - 1):
        outgoing = s_end + (a_end * link)[:, None, None] * prefix
        prefix, got_id = passed_along((outgoing, sent_id), "seq", 1)
        link = (got_id[0] == first_id).astype(jnp.float32)
    back = jnp.zeros_like(s_end)
    for turn in range(count - 1):
        back = passed_along(link * (grad_in + a_end[:, None, None] * back), "seq", -1)
    h_in = link * prefix

    def local(p_in, x_in):
        return span_forward(p_in, x_in, id_row, a_log, dt_bias, d_skip, h_in)

    (y_full, h_out), pull = jax.vjp(local, proj, xf)
    d_proj, d_x = pull((dyf, back))
    d_round = d_proj.astype(jnp.bfloat16)
    d_u = jnp.dot(d_round, weights.T, preferred_element_type=jnp.float32)
    partial_w = lax.dot_general(
        u_rows, d_round, (((0,), (0,)), ((), ())), preferred_element_type=jnp.float32
    )
    summed = lax.psum(partial_w, "seq")
    grad_w = lax.psum_scatter(summed, "dp", scatter_dimension=0, tiled=True)
    return (
        y_full.astype(jnp.bfloat16)[None],
        d_x.astype(jnp.bfloat16)[None],
        d_u.astype(jnp.bfloat16)[None],
        grad_w,
    )


def solution(mesh):
    return jax.shard_map(
        body,
        mesh=mesh,
        in_specs=(
            P("dp", "seq", None),
            P("dp", "seq", None),
            P("dp", "seq"),
            P("dp", "seq", None),
            P("dp", None),
            P(),
            P(),
            P(),
        ),
        out_specs=(P("dp", "seq", None), P("dp", "seq", None), P("dp", "seq", None), P("dp", None)),
        check_vma=False,
    )
```

profile of v0, /device:TPU:8, one launch (start us, length us, event | category | flops | bytes accessed | tf_op | source)
XLA Modules:
  0.0 644.5 jit_solution(12199185451268589756)
XLA Ops:
  9.9 4.7 collective-permute-start
  17.2 4.1 copy.91
  23.3 67.6 %all-gather.2.cloned.1.call-done = bf16[4096,320]{1,0:T(8,128)(2,1)} async-done(((bf16[64,320]{1,0:T(8,128)(2,1)}), bf16[4096,320]{1,0:T(8,128)(2,1)}) %all-gather.2.cloned.1.call-update) | async-done | bytes 2621456 | tf_op jit(solution)/shard_map/all_gather | solution.py:62
  90.8 3.2 fusion.37
  95.6 5.2 add_multiply_fusion.2
  102.0 48.4 %collective-permute-done.4 = f32[64,64,128]{2,1,0:T(8,128)S(1)} collective-permute-done((f32[64,64,128]{2,1,0:T(8,128)S(1)}, f32[64,64,128]{2,1,0:T(8,128)S(1)}, u32[]{:S(2)}, u32[]{:S(2)}) %collective-permute-start.4) | collective-permute-done | bytes 2097184 | tf_op jit(solution)/shard_map/ppermute | solution.py:10
  152.0 47.6 %collective-permute-done.5 = f32[64,64,128]{2,1,0:T(8,128)S(1)} collective-permute-done((f32[64,64,128]{2,1,0:T(8,128)S(1)}, f32[64,64,128]{2,1,0:T(8,128)S(1)}, u32[]{:S(2)}, u32[]{:S(2)}) %collective-permute-start.5) | collective-permute-done | bytes 2097184 | tf_op jit(solution)/shard_map/ppermute | solution.py:10
  203.0 4.1 copy.86
  207.1 42.4 %collective-permute-done.6 = f32[64,64,128]{2,1,0:T(8,128)} collective-permute-done((f32[64,64,128]{2,1,0:T(8,128)}, f32[64,64,128]{2,1,0:T(8,128)}, u32[]{:S(2)}, u32[]{:S(2)}) %collective-permute-start.6) | collective-permute-done | bytes 2097184 | tf_op jit(solution)/shard_map/ppermute | solution.py:10
  249.5 7.9 %fusion.27 = (f32[256,64]{0,1:T(8,128)S(1)}, f32[256,64,64]{0,2,1:T(8,128)}) fusion(bf16[256,64,64]{0,2,1:T(8,128)(2,1)} %bitcast.119, f32[64,64,128]{2,1,0:T(8,128)} %collective-permute-done.6, f32[256,320]{0,1:T(8,128)S(1)} %fusion.37), kind=kOutput, calls=%fused_computation.37 | convolution fusion | flops 1613742080 | bytes 8585216 | tf_op jit(solution)/shard_map/transpose(jvp(thp,tn->hpn))/dot_general | solution.py:34
  258.2 5.2 broadcast_add_fusion
  263.4 3.5 collective-permute-start.1
  266.9 42.5 %collective-permute-done.1 = f32[64,64,128]{2,1,0:T(8,128)S(1)} collective-permute-done((f32[64,64,128]{2,1,0:T(8,128)S(1)}, f32[64,64,128]{2,1,0:T(8,128)S(1)}, u32[]{:S(2)}, u32[]{:S(2)}) %collective-permute-start.1) | collective-permute-done | bytes 2097184 | tf_op jit(solution)/shard_map/ppermute | solution.py:10
  311.1 5.7 collective-permute-start.2
  318.8 38.7 %collective-permute-done.2 = f32[64,64,128]{2,1,0:T(8,128)} collective-permute-done((f32[64,64,128]{2,1,0:T(8,128)}, f32[64,64,128]{2,1,0:T(8,128)}, u32[]{:S(2)}, u32[]{:S(2)}) %collective-permute-start.2) | collective-permute-done | bytes 2097184 | tf_op jit(solution)/shard_map/ppermute | solution.py:10
  357.5 3.8 multiply_add_fusion
  361.3 5.7 collective-permute-start.3
  367.1 12.1 %fusion.7 = (f32[64,256]{1,0:T(8,128)}, f32[64,256]{1,0:T(8,128)}, f32[64,256]{1,0:T(8,128)}, f32[256,256]{1,0:T(8,128)S(1)}) fusion(f32[64,256]{1,0:T(8,128)S(1)} %copy-done.12, f32[256,256]{1,0:T(8,128)S(1)} %fusion.70, f32[64,256]{1,0:T(8,128)S(1)} %copy.83, pred[256,256]{1,0:T(8,128)(4,1)S(1)} %copy-done.14, bf16[64,64,256]{2,1,0:T(8,128)(2,1)S(1)} %bitcast.115, ...), kind=kOutput, calls=%fused_computation.9 | convolution fusion | flops 591282176 | bytes 5111808 | tf_op jit(solution)/shard_map/transpose(jvp(hts,shp->thp))/dot_general | solution.py:27
  384.3 8.9 %fusion.50 = f32[256,128]{1,0:T(8,128)S(1)} fusion(f32[256,128]{1,0:T(8,128)S(1)} %fusion.73, f32[64,64,128]{2,1,0:T(8,128)} %collective-permute-done.6, bf16[256,64,64]{0,2,1:T(8,128)(2,1)} %bitcast.121, f32[256,64]{0,1:T(8,128)S(1)} %copy.88), kind=kOutput, calls=%fused_computation.61 | convolution fusion | flops 1612742656 | bytes 4521984 | tf_op jit(solution)/shard_map/transpose(jvp(thp,tn->hpn))/dot_general | solution.py:34
  393.3 13.6 %collective-permute-done.3 = f32[64,64,128]{2,1,0:T(8,128)} collective-permute-done((f32[64,64,128]{2,1,0:T(8,128)}, f32[64,64,128]{2,1,0:T(8,128)}, u32[]{:S(2)}, u32[]{:S(2)}) %collective-permute-start.3) | collective-permute-done | bytes 2097184 | tf_op jit(solution)/shard_map/ppermute | solution.py:10
  406.8 2.8 multiply_reduce_fusion.2
  410.1 7.3 %fusion.31 = (f32[256,64]{0,1:T(8,128)S(1)}, f32[256,64,64]{0,2,1:T(8,128)}) fusion(bf16[256,64,64]{0,2,1:T(8,128)(2,1)S(1)} %bitcast.116, f32[64,64,128]{2,1,0:T(8,128)} %collective-permute-done.3, f32[]{:T(128)S(6)} %convert_element_type.78, f32[256,320]{0,1:T(8,128)S(1)} %fusion.37), kind=kOutput, calls=%fused_computation.41 | convolution fusion | flops 1614266368 | bytes 8585220 | tf_op jit(solution)/shard_map/jvp(tn,hpn->thp)/dot_general | solution.py:30
  422.6 9.0 %fusion.51 = f32[256,128]{1,0:T(8,128)S(1)} fusion(f32[256,128]{1,0:T(8,128)} %fusion.67, f32[64,64,128]{2,1,0:T(8,128)} %collective-permute-done.3, bf16[256,64,64]{0,2,1:T(8,128)(2,1)} %bitcast.114, f32[256,64]{0,1:T(8,128)S(1)} %copy.87, f32[]{:T(128)S(6)} %convert_element_type.78), kind=kOutput, calls=%fused_computation.62 | convolution fusion | flops 1613266944 | bytes 4521988 | tf_op jit(solution)/shard_map/transpose(jvp(tn,hpn->thp))/dot_general | solution.py:30
  431.5 3.3 convolution_bitcast_fusion
  434.8 6.3 copy.123
  442.8 13.6 %fusion.30 = bf16[256,64,64]{0,2,1:T(8,128)(2,1)} fusion(bf16[256,64,64]{0,2,1:T(8,128)(2,1)S(1)} %bitcast.117, f32[256,64,64]{0,2,1:T(8,128)} %get-tuple-element.40, bf16[64,64,256]{2,1,0:T(8,128)(2,1)S(1)} %bitcast.118, f32[64,256]{1,0:T(8,128)S(1)} %copy-done.13, f32[256,256]{1,0:T(8,128)S(1)} %copy-done.9, f32[64,256]{1,0:T(8,128)S(1)} %copy-done.11, ...), kind=kOutput, calls=%fused_computation.40 | convolution fusion | flops 3244294144 | bytes 11010304 | tf_op jit(solution)/shard_map/transpose(jvp(hts,shp->thp))/dot_general | solution.py:27
  456.4 4.3 copy.107
  460.6 15.6 %fusion.26 = bf16[256,64,64]{0,2,1:T(8,128)(2,1)} fusion(bf16[256,64,64]{0,2,1:T(8,128)(2,1)S(1)} %bitcast.123, f32[256,64,64]{0,2,1:T(8,128)} %get-tuple-element.44, f32[64,256]{1,0:T(8,128)S(1)} %copy-done.13, f32[256,256]{1,0:T(8,128)S(1)} %copy-done.9, f32[64,256]{1,0:T(8,128)S(1)} %copy-done.11, pred[256,256]{1,0:T(8,128)(4,1)S(1)} %copy-done.15, ...), kind=kOutput, calls=%fused_computation.36 | convolution fusion | flops 3244294144 | bytes 8913152 | tf_op jit(solution)/shard_map/jvp(hts,shp->thp)/dot_general | solution.py:27
  476.2 111.8 %reduce-scatter.4.cloned.1.call-done = f32[64,320]{1,0:T(8,128)} async-done(((f32[4096,320]{1,0:T(8,128)}), f32[64,320]{1,0:T(8,128)}) %reduce-scatter.4.cloned.1.call-update) | async-done | bytes 81936
  589.7 4.5 fusion.24
  594.2 4.2 copy.106
  598.5 37.6 %all-reduce.7.cloned.1.call-done = f32[64,320]{0,1:T(8,128)} async-done(((f32[64,320]{0,1:T(8,128)}), f32[64,320]{0,1:T(8,128)}) %all-reduce.7.cloned.1.call-update) | async-done | bytes 81936 | tf_op jit(solution)/shard_map/psum | solution.py:97
  (98 shorter events, 31.8 us)
Async XLA Ops:
  7.2 83.7 %copy-start = (bf16[1,256,4096]{2,1,0:T(8,128)(2,1)S(1)}, bf16[1,256,4096]{2,1,0:T(8,128)(2,1)}, u32[]{:S(2)}) copy-start(bf16[1,256,4096]{2,1,0:T(8,128)(2,1)} %param.8) | copy-start | bytes 6291460
  7.2 83.7 %all-gather.2.cloned.1.call-start = ((), (), s32[]{:S(2)}) async-start(), calls=%async_computation.1 | async-start | bytes 3194880 | tf_op jit(solution)/shard_map/all_gather | solution.py:62
  7.9 580.1 %reduce-scatter.4.cloned.1.call-start = ((), (), s32[]{:S(2)}) async-start(), calls=%async_computation.3 | async-start | bytes 6389760
  9.9 12.7 %collective-permute-start = (f32[1]{0:T(128)}, f32[1]{0:T(128)}, u32[]{:S(2)}, u32[]{:S(2)}) collective-permute-start(f32[1]{0:T(128)} %bitcast.12), channel_id=1, source_target_pairs={{0,1},{1,2},{2,3},{4,5},{5,6},{6,7},{8,9},{9,10},{10,11},{12,13},{... | collective-permute-start | bytes 20 | tf_op jit(solution)/shard_map/ppermute | solution.py:10
  17.2 77.0 %copy-start.19 = (f32[64]{0:T(128)}, f32[64]{0:T(128)S(1)}, u32[]{:S(2)}) copy-start(f32[64]{0:T(128)S(1)} %exp.43) | copy-start | bytes 772
  17.2 4.1 copy-start.16
  23.3 70.9 %copy-start.17 = (f32[64]{0:T(128)S(1)}, f32[64]{0:T(128)}, u32[]{:S(2)}) copy-start(f32[64]{0:T(128)} %param.14) | copy-start | bytes 772
  95.4 214.1 %copy-start.18 = (f32[64]{0:T(128)}, f32[64]{0:T(128)S(1)}, u32[]{:S(2)}) copy-start(f32[64]{0:T(128)S(1)} %get-tuple-element.28) | copy-start | bytes 772
  100.7 49.7 %collective-permute-start.4 = (f32[64,64,128]{2,1,0:T(8,128)S(1)}, f32[64,64,128]{2,1,0:T(8,128)S(1)}, u32[]{:S(2)}, u32[]{:S(2)}) collective-permute-start(f32[64,64,128]{2,1,0:T(8,128)S(1)} %get-tuple-element.37), channel_id=1, source_target_pairs={{1,0},{2,1},{3,2},{5,4},{6,5},{7,6},{9,8},{10,9},{11,10},{13,12},{... | collective-permute-start | bytes 6291464 | tf_op jit(solution)/shard_map/ppermute | solution.py:10
  150.7 48.9 %collective-permute-start.5 = (f32[64,64,128]{2,1,0:T(8,128)S(1)}, f32[64,64,128]{2,1,0:T(8,128)S(1)}, u32[]{:S(2)}, u32[]{:S(2)}) collective-permute-start(f32[64,64,128]{2,1,0:T(8,128)S(1)} %add_multiply_fusion.1), channel_id=1, source_target_pairs={{1,0},{2,1},{3,2},{5,4},{6,5},{7,6},{9,8},{10,9},{11,10},{13,12},{... | collective-permute-start | bytes 6291464 | tf_op jit(solution)/shard_map/ppermute | solution.py:10
  201.2 48.3 %collective-permute-start.6 = (f32[64,64,128]{2,1,0:T(8,128)}, f32[64,64,128]{2,1,0:T(8,128)}, u32[]{:S(2)}, u32[]{:S(2)}) collective-permute-start(f32[64,64,128]{2,1,0:T(8,128)} %add_multiply_fusion), channel_id=1, source_target_pairs={{1,0},{2,1},{3,2},{5,4},{6,5},{7,6},{9,8},{10,9},{11,10},{13,12},{... | collective-permute-start | bytes 6291464 | tf_op jit(solution)/shard_map/ppermute | solution.py:10
  263.4 47.7 %copy-start.7 = (f32[64,64,128]{2,1,0:T(8,128)}, f32[64,64,128]{2,1,0:T(8,128)S(1)}, u32[]{:S(2)}) copy-start(f32[64,64,128]{2,1,0:T(8,128)S(1)} %get-tuple-element.42) | copy-start | bytes 6291460
  263.4 46.0 %collective-permute-start.1 = (f32[64,64,128]{2,1,0:T(8,128)S(1)}, f32[64,64,128]{2,1,0:T(8,128)S(1)}, u32[]{:S(2)}, u32[]{:S(2)}) collective-permute-start(f32[64,64,128]{2,1,0:T(8,128)S(1)} %get-tuple-element.41), channel_id=1, source_target_pairs={{0,1},{1,2},{2,3},{4,5},{5,6},{6,7},{8,9},{9,10},{10,11},{12,13},{... | collective-permute-start | bytes 6291464 | tf_op jit(solution)/shard_map/ppermute | solution.py:10
  311.1 46.4 %collective-permute-start.2 = (f32[64,64,128]{2,1,0:T(8,128)}, f32[64,64,128]{2,1,0:T(8,128)}, u32[]{:S(2)}, u32[]{:S(2)}) collective-permute-start(f32[64,64,128]{2,1,0:T(8,128)} %multiply_add_fusion.1), channel_id=1, source_target_pairs={{0,1},{1,2},{2,3},{4,5},{5,6},{6,7},{8,9},{9,10},{10,11},{12,13},{... | collective-permute-start | bytes 6291464 | tf_op jit(solution)/shard_map/ppermute | solution.py:10
  317.6 49.4 %copy-start.10 = (f32[64,256]{1,0:T(8,128)}, f32[64,256]{1,0:T(8,128)S(1)}, u32[]{:S(2)}) copy-start(f32[64,256]{1,0:T(8,128)S(1)} %copy.83) | copy-start | bytes 196612
  318.0 49.0 %copy-start.8 = (f32[256,256]{1,0:T(8,128)}, f32[256,256]{1,0:T(8,128)S(1)}, u32[]{:S(2)}) copy-start(f32[256,256]{1,0:T(8,128)S(1)} %fusion.70) | copy-start | bytes 786436
  318.8 48.3 %copy-start.2 = (bf16[1,256,4096]{1,2,0:T(8,128)(2,1)S(1)}, bf16[1,256,4096]{1,2,0:T(8,128)(2,1)}, u32[]{:S(2)}) copy-start(bf16[1,256,4096]{1,2,0:T(8,128)(2,1)} %copy.91) | copy-start | bytes 6291460
  318.8 48.3 %copy-start.5 = (bf16[1,256,4096]{1,2,0:T(8,128)(2,1)S(1)}, bf16[1,256,4096]{1,2,0:T(8,128)(2,1)}, u32[]{:S(2)}) copy-start(bf16[1,256,4096]{1,2,0:T(8,128)(2,1)} %copy.86) | copy-start | bytes 6291460
  318.8 48.3 %copy-start.12 = (f32[64,256]{1,0:T(8,128)S(1)}, f32[64,256]{1,0:T(8,128)}, u32[]{:S(2)}) copy-start(f32[64,256]{1,0:T(8,128)} %copy.85) | copy-start | bytes 196612
  318.8 48.3 %copy-start.14 = (pred[256,256]{1,0:T(8,128)(4,1)S(1)}, pred[256,256]{1,0:T(8,128)(4,1)}, u32[]{:S(2)}) copy-start(pred[256,256]{1,0:T(8,128)(4,1)} %fusion.56) | copy-start | bytes 196612
  361.3 45.5 %collective-permute-start.3 = (f32[64,64,128]{2,1,0:T(8,128)}, f32[64,64,128]{2,1,0:T(8,128)}, u32[]{:S(2)}, u32[]{:S(2)}) collective-permute-start(f32[64,64,128]{2,1,0:T(8,128)} %multiply_add_fusion), channel_id=1, source_target_pairs={{0,1},{1,2},{2,3},{4,5},{5,6},{6,7},{8,9},{9,10},{10,11},{12,13},{... | collective-permute-start | bytes 6291464 | tf_op jit(solution)/shard_map/ppermute | solution.py:10
  393.2 16.9 %copy-start.3 = (bf16[1,256,4096]{1,2,0:T(8,128)(2,1)S(1)}, bf16[1,256,4096]{1,2,0:T(8,128)(2,1)}, u32[]{:S(2)}) copy-start(bf16[1,256,4096]{1,2,0:T(8,128)(2,1)} %copy.91) | copy-start | bytes 6291460
  441.1 1.6 copy-start.4
  441.1 1.6 copy-start.9
  441.1 1.6 copy-start.11
  441.1 1.6 copy-start.13
  441.2 1.6 copy-start.15
  441.2 1.6 copy-start.20
  441.2 194.8 %all-reduce.7.cloned.1.call-start = ((), (), s32[]{:S(2)}) async-start(), calls=%async_computation.2 | async-start | bytes 327680 | tf_op jit(solution)/shard_map/psum | solution.py:97
  456.4 4.3 copy-start.6
  594.2 43.5 %copy-start.1 = (bf16[1,256,4096]{2,1,0:T(8,128)(2,1)S(1)}, bf16[1,256,4096]{2,1,0:T(8,128)(2,1)}, u32[]{:S(2)}) copy-start(bf16[1,256,4096]{2,1,0:T(8,128)(2,1)} %param.8) | copy-start | bytes 6291460
Sparse Core Ops, SparseCore 0:
  10.8 80.0 all-gather.1
  441.3 146.6 reduce-scatter.3
  590.5 45.4 all-reduce.6
where the time goes:
time: 651 us; the launch traced here: 644 us
  waiting for transfers between devices  451 us (69%)
  matrix products  97.7 us (15%)
  local copies, waits for them, and re-layouts  35.1 us (5%)
  starting transfers between devices  24.2 us (4%)
  other arithmetic  19 us (3%)
  between operations  17.7 us (3%)
    ppermute x7, waiting for transfers between devices, passed_along(): lax.ppermute(value, axis, [(source, source + steps) for source in range(l...  233 us
    unnamed x4, waiting for transfers between devices  113 us
    all_gather x1, waiting for transfers between devices, body(): weights = lax.all_gather(w_in, 'dp', axis=0, tiled=True)  67.6 us
    dot_general x3, matrix products, span_forward(): jnp.einsum('hts,shp->thp', mixing, xh, precision=lax.Precision.HIGHEST)  41.3 us
    psum x1, waiting for transfers between devices, body(): summed = lax.psum(partial_w, 'seq')  37.6 us
    unnamed x50, local copies, waits for them, and re-layouts  28 us
    ppermute x7, starting transfers between devices, passed_along(): lax.ppermute(value, axis, [(source, source + steps) for source in range(l...  24.1 us
    dot_general x2, matrix products, span_forward(): jnp.einsum('thp,tn->hpn', xh * end_w[:, :, None], b_mat, precision=lax.Pr...  16.8 us
  transfers between devices with their start and end apart: 10, of which 9 were waited for; matrix products, arithmetic and copies ran while one was open for 13% of the time, Pallas kernels for 0%

commit v1 on v0

v1 whole, which is shorter than its diff:
```python
import functools

import jax
import jax.numpy as jnp
from jax import lax
from jax.experimental import pallas as pl
from jax.experimental.pallas import tpu as pltpu
from jax.sharding import PartitionSpec as P

bf16, f32 = jnp.bfloat16, jnp.float32
NY, NZ, NC, NX = 4, 8, 2, 4
T, L, D, H, PS, N, PROJ = 256, 128, 4096, 64, 64, 128, 320
GL, GH = 512, 8
PL = 1024
VMEM = functools.partial(pl.BlockSpec, memory_space=pltpu.VMEM)
SMEM = functools.partial(pl.BlockSpec, memory_space=pltpu.SMEM)
PARAMS = pltpu.CompilerParams(vmem_limit_bytes=60 * 1024 * 1024)
SMALL = pltpu.CompilerParams(vmem_limit_bytes=20 * 1024 * 1024)
ANY = pl.BlockSpec(memory_space=pl.ANY)
HIGHEST = lax.Precision.HIGHEST
COST = pl.CostEstimate(flops=1 << 20, bytes_accessed=1 << 16, transcendentals=0)


def fetch(value, source):
    pairs = []
    for y in range(NY):
        for z in range(NZ):
            for c in range(NC):
                for x in range(NX):
                    sy, sz, sc, sx = source(y, z, c, x)
                    at = ((sy % NY * NZ + sz % NZ) * NC + sc % NC) * NX + sx % NX
                    pairs.append((at, ((y * NZ + z) * NC + c) * NX + x))
    return lax.ppermute(value, ("dp", "seq"), pairs)


def shift(value, dy=0, dz=0, dc=0, dx=0):
    return fetch(value, lambda y, z, c, x: (y + dy, z + dz, c + dc, x + dx))


def from_seq(value, offset):
    pairs = [(s + offset, s) for s in range(NX) if 0 <= s + offset < NX]
    return lax.ppermute(value, "seq", pairs)


def dot(a, b, dims=((1,), (0,)), precision=None):
    return lax.dot_general(
        a, b, (dims, ((), ())), preferred_element_type=f32, precision=precision
    )


def parts(value, count):
    out, rest = [], value
    for _ in range(count):
        piece = rest.astype(bf16)
        out.append(piece)
        rest = rest - piece.astype(f32)
    return out


def expand(value, ind, count=2):
    return sum(dot(piece, ind) for piece in parts(value, count))


def head_lanes(first_head, copies, lanes, shift_bits):
    rows = lax.broadcasted_iota(jnp.int32, (copies * H, lanes), 0)
    cols = lax.broadcasted_iota(jnp.int32, (copies * H, lanes), 1)
    return ((rows & (H - 1)) == (cols >> shift_bits) + first_head).astype(f32).astype(bf16)


def lanes_head(first_head, lanes):
    rows = lax.broadcasted_iota(jnp.int32, (lanes, H), 0)
    cols = lax.broadcasted_iota(jnp.int32, (lanes, H), 1)
    return (cols == (rows >> 6) + first_head).astype(f32).astype(bf16)


def put_parts(ref, value, count):
    width = value.shape[1]
    for i, piece in enumerate(parts(value, count)):
        ref[:, i * width : (i + 1) * width] = piece


ORDER = (7, 0, 1, 2, 3, 4, 5, 6)
PLAN = ((0, 0, 8), (1, 0, 8), (3, 0, 8), (2, 0, 4), (2, 4, 8))


def prep_kernel(pos, u, x_hbm, dy_hbm, idc, a_log, dt_bias, d_skip, *refs):
    pieces, outs = refs[:10], refs[10:]
    (w_abs, b_out, c_out, bb_out, cc_out, sig_out, stept_out, cumt_out,
     cum3, ew2, re2, cross2, vecs, s_end, g_in, link_out, linkn_out, x, dy, sems) = outs
    copies = [
        pltpu.make_async_copy(source, target, sems.at[i])
        for i, (source, target) in enumerate(((x_hbm, x), (dy_hbm, dy)))
    ]
    for copy in copies:
        copy.start()
    my_y, my_z, my_c = pos[0], pos[1], pos[2]
    for core in range(2):
        for (yo, lo, hi), piece in zip(PLAN, pieces[5 * core : 5 * core + 5]):
            for k in range(lo, hi):
                owner = (
                    lax.rem(my_y + yo, NY) * NZ + lax.rem(my_z + ORDER[k], NZ)
                ) * NC + lax.rem(my_c + core, NC)
                w_abs[pl.ds(pl.multiple_of(owner * 64, 64), 64), :] = piece[
                    (k - lo) * 64 : (k - lo + 1) * 64, :
                ]
    proj = dot(u[...], w_abs[...])
    b, c = proj[:, :N], proj[:, N : 2 * N]
    z = proj[:, 2 * N :] + dt_bias[...]
    small = jnp.exp(-jnp.abs(z))
    step = jnp.maximum(z, 0.0) + jnp.log1p(small)
    sig = jnp.where(z >= 0, 1.0, small) / (1.0 + small)
    sig_out[:, :H] = sig
    tiny = step < 1e-30
    sig_out[:, H:] = jnp.where(tiny, 1.0, sig / jnp.where(tiny, 1.0, step))
    la = -step * jnp.exp(a_log[...])
    rows = lax.broadcasted_iota(jnp.int32, (T, T), 0)
    cols = lax.broadcasted_iota(jnp.int32, (T, T), 1)
    tril = (rows >= cols).astype(f32).astype(bf16)
    cum = sum(dot(tril, piece) for piece in parts(la, 3))
    ids = idc[...]
    id0, idm, ide = ids[0:1], ids[L - 1 : L], ids[T - 1 : T]
    nxt, prv = pieces[3][256:257, 0:1].astype(f32), pieces[4][256:257, 0:1].astype(f32)
    link = jnp.where((prv == id0.astype(f32)) & (pos[3] > 0), 1.0, 0.0)
    linkn = jnp.where((nxt == ide.astype(f32)) & (pos[3] < NX - 1), 1.0, 0.0)
    link_out[...] = link
    linkn_out[...] = linkn
    cm, ce = cum[L - 1 : L], cum[T - 1 : T]
    reach = (ids == id0).astype(f32) * jnp.exp(cum)
    end_w = (ids == ide).astype(f32) * jnp.exp(ce - cum) * step
    put_parts(ew2, end_w, 2)
    put_parts(re2, reach, 2)
    a_end = (id0 == ide).astype(f32) * jnp.exp(ce)
    vec = jnp.concatenate(
        [a_end * link, a_end * linkn, a_end, d_skip[...]] * 2, axis=0
    )
    vec_parts = parts(vec, 3)
    put_parts(bb_out, b, 2)
    put_parts(cc_out, c, 2)
    bt = [piece.astype(bf16) for piece in parts(b.T, 2)]
    ct = [piece.astype(bf16) for piece in parts(c.T, 2)]
    for copy in copies:
        copy.wait()
    for g in range(H // GH):
        lanes = slice(g * GL, (g + 1) * GL)
        ind = head_lanes(g * GH, 2, GL, 6)
        xw = (x[:, lanes].astype(f32) * dot(ew2[...], ind)).astype(bf16)
        s_end[:, lanes] = (dot(bt[0], xw) + dot(bt[1], xw)).astype(bf16)
        dyr = (dy[:, lanes].astype(f32) * dot(re2[...], ind)).astype(bf16)
        g_in[:, lanes] = (dot(ct[0], dyr) + dot(ct[1], dyr)).astype(bf16)
        vecs[:, lanes] = sum(dot(piece, ind[:H]) for piece in vec_parts)
    b_out[...] = b
    c_out[...] = c
    stept_out[...] = step.T
    cumt_out[...] = cum.T
    put_parts(cum3, cum, 3)
    late = (ids[L:] == idm).astype(f32) * jnp.exp(cum[L:] - cm)
    early = (ids[:L] == idm).astype(f32) * jnp.exp(cm - cum[:L])
    put_parts(cross2, jnp.concatenate([early * step[:L], late], axis=0), 2)


def prep(pos, u, x, dy, idc, a_log, dt_bias, d_skip, pieces):
    def shape(rows, cols, kind=f32):
        return jax.ShapeDtypeStruct((rows, cols), kind)

    return pl.pallas_call(
        prep_kernel,
        out_shape=(
            shape(D, PROJ, bf16), shape(T, N), shape(T, N), shape(T, 2 * N, bf16),
            shape(T, 2 * N, bf16), shape(T, 2 * H), shape(H, T), shape(H, T),
            shape(T, 3 * H, bf16), shape(T, 2 * H, bf16), shape(T, 2 * H, bf16),
            shape(T, 2 * H, bf16), shape(8, D), shape(N, D, bf16), shape(N, D, bf16),
            shape(1, 1), shape(1, 1),
        ),
        in_specs=[SMEM(), VMEM()] + [pl.BlockSpec(memory_space=pl.ANY)] * 2
        + [VMEM()] * (4 + len(pieces)),
        out_specs=tuple([VMEM()] * 17),
        scratch_shapes=[
            pltpu.VMEM((T, D), bf16), pltpu.VMEM((T, D), bf16), pltpu.SemaphoreType.DMA((2,)),
        ],
        compiler_params=PARAMS,
        cost_estimate=COST,
    )(pos, u, x, dy, idc, a_log, dt_bias, d_skip, *pieces)


def intra_kernel(
    x, dy, cumt, stept, cum3, ew2, re2, cross2, b, c, bb, cc, idc, idr,
    y_out, dx_out, dyr_out, xw_out, d_out, row_out, col_out, ds_out, dbc_out, token, sc,
):
    g = pl.program_id(0)
    rows = lax.broadcasted_iota(jnp.int32, (L, L), 0)
    cols = lax.broadcasted_iota(jnp.int32, (L, L), 1)

    @pl.when(g == 0)
    def _():
        for k in range(2):
            span = slice(k * L, (k + 1) * L)
            scores = dot(c[span, :], b[span, :], ((1,), (1,)), HIGHEST)
            keep = (idc[span, :] == idr[:, span]) & (rows >= cols)
            sc[k] = jnp.where(keep, scores, 0.0)
        for out in (d_out, row_out, col_out, ds_out, dbc_out, token):
            out[...] = jnp.zeros_like(out)

    cum_e = dot(cum3[...], head_lanes(g * GH, 3, GH * L, 7))
    low = lax.broadcasted_iota(jnp.int32, (L, L), 1) < PS
    cumt_g, stept_g = cumt[...], stept[...]
    for k in range(2):
        span = slice(k * L, (k + 1) * L)
        total = jnp.zeros((L, L), f32)
        scores = sc[k]
        for q in range(GH // 2):
            lanes = slice(q * L, (q + 1) * L)
            dyp, xp = dy[span, lanes], x[span, lanes]
            zero = jnp.zeros_like(xp)
            xm = jnp.concatenate([jnp.where(low, xp, zero), jnp.where(low, zero, xp)], axis=0)
            dym = jnp.concatenate([jnp.where(low, dyp, zero), jnp.where(low, zero, dyp)], axis=0)
            grad = dot(dyp, xm, ((1,), (1,)))
            mixing = []
            for half in range(2):
                h = 2 * q + half
                gap = cum_e[span, h * L : (h + 1) * L] - cumt_g[h : h + 1, span]
                e = jnp.exp(jnp.minimum(gap, 0.0)) * stept_g[h : h + 1, span]
                total += e * grad[:, half * L : (half + 1) * L]
                mixing.append((e * scores).astype(bf16))
            y_out[span, lanes] = dot(jnp.concatenate(mixing, axis=1), xm)
            dx_out[span, lanes] = dot(jnp.concatenate(mixing, axis=0), dym, ((0,), (0,)))
        ds_out[k] += total
    ind = head_lanes(g * GH, 2, GL, 6)
    pool = lanes_head(g * GH, GL)

    def pooled(value):
        return sum(dot(piece, pool) for piece in parts(value, 2))

    xf, dyf = x[...].astype(f32), dy[...].astype(f32)
    cross = dot(cross2[...], ind)
    xw = (xf[:L] * cross[:L]).astype(bf16)
    dyr = (dyf[L:] * cross[L:]).astype(bf16)
    state = sum(dot(piece, xw) for piece in parts(b[:L, :].T, 2)).astype(bf16)
    back = sum(dot(piece, dyr) for piece in parts(c[L:, :].T, 2)).astype(bf16)
    last = ((1,), (1,))
    dbc_out[0] += dot(xw, back, last)
    dbc_out[1] += dot(dyr, state, last)
    read = dot(cc[L:, :], twice(state))
    sent = dot(bb[:L, :], twice(back))
    row_out[L:, :] += pooled(dyr.astype(f32) * read)
    far = pooled(xw.astype(f32) * sent)
    col = xf * dx_out[...]
    near = pooled(col)
    d_out[...] += near - pooled(dyf * y_out[...])
    d_out[:L, :] += far
    col_out[...] += near
    col_out[:L, :] += far
    y_out[L:, :] += cross[L:] * read
    dx_out[:L, :] += cross[:L] * sent
    xw_out[...] = (xf * dot(ew2[...], ind)).astype(bf16)
    dyr_out[...] = (dyf * dot(re2[...], ind)).astype(bf16)


def whole(*dims):
    return VMEM(dims, lambda i: (0,) * len(dims))


def block(rows, lanes=GL):
    return VMEM((rows, lanes), lambda i: (0, i))


def twice(value):
    return jnp.concatenate([value, value], axis=0)


def intra(x, dy, cumt, stept, cum3, ew2, re2, cross2, b, c, bb, cc, idc, idr):
    def shape(*dims, kind=f32):
        return jax.ShapeDtypeStruct(dims, kind)

    heads = VMEM((GH, T), lambda i: (i, 0))
    return pl.pallas_call(
        intra_kernel,
        grid=(H // GH,),
        out_shape=(
            shape(T, D), shape(T, D), shape(T, D, kind=bf16), shape(T, D, kind=bf16),
            shape(T, H), shape(T, H), shape(T, H), shape(2, L, L), shape(2, L, N), shape(8, 128),
        ),
        in_specs=[
            block(T), block(T), heads, heads, whole(T, 3 * H), whole(T, 2 * H),
            whole(T, 2 * H), whole(T, 2 * H), whole(T, N), whole(T, N), whole(T, 2 * N),
            whole(T, 2 * N), whole(T, 1), whole(1, T),
        ],
        out_specs=(
            block(T), block(T), block(T), block(T), whole(T, H), whole(T, H), whole(T, H),
            whole(2, L, L), whole(2, L, N), whole(8, 128),
        ),
        scratch_shapes=[pltpu.VMEM((2, L, L), f32)],
        compiler_params=PARAMS,
        cost_estimate=COST,
    )(x, dy, cumt, stept, cum3, ew2, re2, cross2, b, c, bb, cc, idc, idr)


def hop_kernel(one, back, vecs, token, out_one, out_back):
    out_one[...] = (one[...].astype(f32) * vecs[0:1, :]).astype(bf16)
    out_back[...] = (back[...].astype(f32) * vecs[1:2, :]).astype(bf16)


def hop(one, back, vecs, token):
    return pl.pallas_call(
        hop_kernel,
        grid=(D // PL,),
        out_shape=(jax.ShapeDtypeStruct((N, D), bf16),) * 2,
        in_specs=[block(N, PL), block(N, PL), block(8, PL), ANY],
        out_specs=(block(N, PL),) * 2,
        compiler_params=SMALL,
        cost_estimate=COST,
    )(one, back, vecs, token)


def arrived(one, two, link):
    return (link[...] * (one[...].astype(f32) + two[...].astype(f32))).astype(bf16)


def post_kernel(
    r1, r2, b1, b2, dyr, xw, vecs, bb, cc, link, linkn,
    d, row_in, col_in, ds, dbc, sig, b, c, idc, idr, a_log, dround, dlow,
    dc_acc, db_acc, row_acc, col_acc, flow_acc,
):
    g = pl.program_id(0)

    @pl.when(g == 0)
    def _():
        for acc in (dc_acc, db_acc, row_acc, col_acc, flow_acc):
            acc[...] = jnp.zeros_like(acc)

    pool = lanes_head(g * (PL // PS), PL)
    s0, dse = arrived(r1, r2, link), arrived(b1, b2, linkn)
    last = ((1,), (1,))
    dc_acc[...] += dot(dyr[...], s0, last)
    db_acc[...] += dot(xw[...], dse, last)
    read, sent = dot(cc[:, :N], s0), dot(bb[:, :N], dse)
    row_acc[...] += dot((dyr[...].astype(f32) * read).astype(bf16), pool)
    col_acc[...] += dot((xw[...].astype(f32) * sent).astype(bf16), pool)
    flow = vecs[2:3, :] * jnp.sum(s0.astype(f32) * dse.astype(f32), axis=0, keepdims=True)
    flow_acc[...] += sum(dot(piece, pool) for piece in parts(flow, 2))


    @pl.when(g == pl.num_programs(0) - 1)
    def _():
        close(
            dc_acc, db_acc, row_acc, col_acc, flow_acc, d, row_in, col_in, ds, dbc, sig, b, c,
            idc, idr, a_log, dround, dlow,
        )


def close(
    dc, db, row, col, flow, d, row_in, col_in, ds, dbc, sig, b, c, idc, idr, a_log, dround, dlow
):
    rows = lax.broadcasted_iota(jnp.int32, (T, T), 0)
    cols = lax.broadcasted_iota(jnp.int32, (T, T), 1)
    same = (rows >> 7) == (cols >> 7)

    def mask(value):
        return value.astype(f32).astype(bf16)

    def total(where, value, count):
        return sum(dot(mask(where), piece) for piece in parts(value, count))

    dla = total(same & (rows > cols), d[...], 3) + total(same & (rows <= cols), row_in[...], 3)
    dla += total(rows > cols, col[...], 3) + total(rows <= cols, row[...], 3) + flow[...]

    def put(span, lanes, value):
        dround[span, lanes] = value.astype(bf16)
        dlow[span, lanes] = (value - value.astype(bf16).astype(f32)).astype(bf16)

    direct = (col_in[...] + col[...]) * sig[:, H:]
    put(slice(0, T), slice(2 * N, PROJ), direct - dla * jnp.exp(a_log[...]) * sig[:, :H])
    rows = lax.broadcasted_iota(jnp.int32, (L, L), 0)
    cols = lax.broadcasted_iota(jnp.int32, (L, L), 1)
    for k in range(2):
        span = slice(k * L, (k + 1) * L)
        keep = (idc[span, :] == idr[:, span]) & (rows >= cols)
        kept = jnp.where(keep, ds[k], 0.0)
        to_b = dot(kept, c[span, :], ((0,), (0,)), HIGHEST) + db[span, :]
        to_c = dot(kept, b[span, :], precision=HIGHEST) + dc[span, :]
        if k == 0:
            to_b += dbc[0]
        else:
            to_c += dbc[1]
        put(span, slice(0, N), to_b)
        put(span, slice(N, 2 * N), to_c)


def post(*args):
    def lanes(rows):
        return block(rows, PL)

    return pl.pallas_call(
        post_kernel,
        grid=(D // PL,),
        out_shape=(jax.ShapeDtypeStruct((T, PROJ), bf16), jax.ShapeDtypeStruct((T, PROJ), bf16)),
        in_specs=[lanes(N)] * 4 + [lanes(T)] * 2 + [
            lanes(8), whole(T, 2 * N), whole(T, 2 * N), whole(1, 1), whole(1, 1),
            whole(T, H), whole(T, H), whole(T, H), whole(2, L, L), whole(2, L, N),
            whole(T, 2 * H), whole(T, N), whole(T, N), whole(T, 1), whole(1, T), whole(1, H),
        ],
        out_specs=(whole(T, PROJ), whole(T, PROJ)),
        scratch_shapes=[
            pltpu.VMEM((T, N), f32), pltpu.VMEM((T, N), f32), pltpu.VMEM((T, H), f32),
            pltpu.VMEM((T, H), f32), pltpu.VMEM((1, H), f32),
        ],
        compiler_params=SMALL,
        cost_estimate=COST,
    )(*args)


def gradw_kernel(pos, ua, ub, da, db, g0, g1, g3, g2a, g2b):
    my_y, my_z = pos[0], pos[1]
    for out, (yo, lo, hi) in zip((g0, g1, g3, g2a, g2b), PLAN):
        for k in range(lo, hi):
            chip = lax.rem(my_y + yo, NY) * NZ + lax.rem(my_z + ORDER[k], NZ)
            at = pl.ds(pl.multiple_of(chip * 64, 64), 64)
            rows = dot(ua[at, :], da[...]) + dot(ub[at, :], db[...])
            out[(k - lo) * 64 : (k - lo + 1) * 64, :] = rows.astype(out.dtype)


def gradw(pos, ua, ub, da, db):
    def shape(rows, kind=bf16):
        return jax.ShapeDtypeStruct((rows, PROJ), kind)

    return pl.pallas_call(
        gradw_kernel,
        out_shape=(shape(512, f32), shape(512), shape(512), shape(256), shape(256)),
        in_specs=[SMEM()] + [VMEM()] * 4,
        out_specs=tuple([VMEM()] * 5),
        compiler_params=SMALL,
        cost_estimate=COST,
    )(pos, ua, ub, da, db)


def gradu_kernel(dhi, dlo, w, out_u, token):
    token[...] = jnp.zeros_like(token)
    last = ((1,), (1,))
    out_u[...] = (dot(dhi[...], w[...], last) + dot(dlo[...], w[...], last)).astype(bf16)


def gradu(dhi, dlo, w):
    return pl.pallas_call(
        gradu_kernel,
        grid=(D // PL,),
        out_shape=(jax.ShapeDtypeStruct((T, D), bf16), jax.ShapeDtypeStruct((8, 128), f32)),
        in_specs=[whole(T, PROJ), whole(T, PROJ), VMEM((PL, PROJ), lambda i: (i, 0))],
        out_specs=(block(T, PL), whole(8, 128)),
        compiler_params=SMALL,
        cost_estimate=COST,
    )(dhi, dlo, w)


def finish_kernel(
    r1, r2, b1, b2, vecs, bb, cc, link, linkn, x, dy, y, dx, ew2, re2, after, out_y, out_x, token
):
    token[...] = jnp.zeros_like(token)
    ind = head_lanes(pl.program_id(0) * GH, 2, GL, 6)
    s0, dse = arrived(r1, r2, link), arrived(b1, b2, linkn)
    skip = vecs[3:4, :]
    y_off = dot(re2[...], ind) * dot(cc[...], twice(s0))
    out_y[...] = (y[...] + y_off + skip * x[...].astype(f32)).astype(bf16)
    dx_off = dot(ew2[...], ind) * dot(bb[...], twice(dse))
    out_x[...] = (dx[...] + dx_off + skip * dy[...].astype(f32)).astype(bf16)


def finish(*args):
    shape = jax.ShapeDtypeStruct((T, D), bf16)
    return pl.pallas_call(
        finish_kernel,
        grid=(H // GH,),
        out_shape=(shape,) * 2 + (jax.ShapeDtypeStruct((8, 128), f32),),
        in_specs=[block(N)] * 4 + [
            block(8), whole(T, 2 * N), whole(T, 2 * N), whole(1, 1), whole(1, 1),
            block(T), block(T), block(T), block(T), whole(T, 2 * H), whole(T, 2 * H), ANY,
        ],
        out_specs=(block(T),) * 2 + (whole(8, 128),),
        compiler_params=SMALL,
        cost_estimate=COST,
    )(*args)


def sum_y_kernel(own, up, down, far_a, far_b, token, near, out_up, out_down):
    total = own[...] + up[...].astype(f32) + down[...].astype(f32)
    total += jnp.concatenate([far_a[...], far_b[...]], axis=0).astype(f32)
    near[...] = total[:192]
    out_up[...] = total[192:384].astype(bf16)
    out_down[...] = total[384:].astype(bf16)


def sum_z_kernel(near, up, down, token, here, left, right):
    left[...] = (near[:64] + up[:64].astype(f32)).astype(bf16)
    here[...] = near[64:128] + up[64:128].astype(f32) + down[:64].astype(f32)
    right[...] = (near[128:] + up[128:].astype(f32) + down[64:].astype(f32)).astype(bf16)


def sums(kernel, outs, args, token):
    return pl.pallas_call(
        kernel,
        out_shape=tuple(jax.ShapeDtypeStruct((rows, PROJ), kind) for rows, kind in outs),
        in_specs=[VMEM()] * len(args) + [ANY],
        out_specs=tuple([VMEM()] * len(outs)),
        compiler_params=SMALL,
        cost_estimate=COST,
    )(*args, token)


def body(layer_in, head_in, ids, dy, w_in, a_log, dt_bias, d_skip):
    u, x, dyv = layer_in[0], head_in[0], dy[0]
    dp, seq = lax.axis_index("dp"), lax.axis_index("seq")
    my_y = (dp // (NZ * NC) + 2 * (seq % 2)) % NY
    pos = jnp.stack([my_y, (dp // NC) % NZ, dp % NC, seq]).astype(jnp.int32)
    idc, idr = ids.reshape(T, 1), ids.reshape(1, T)
    a_log, dt_bias, d_skip = (v.reshape(1, H) for v in (a_log, dt_bias, d_skip))

    def start(k):
        return fetch(w_in, lambda y, z, c, x: (y + 2 * (x % 2), z + k, c, x))

    near = [start(-1), start(0), start(1)]
    near, u, pos, idc = lax.optimization_barrier((near, u, pos, idc))
    near = jnp.concatenate(near, axis=0)
    high, low = shift(near, dz=3), shift(near[64:], dz=-3)

    split = u.reshape(T, NY * NZ, NC, 64)
    mine = lax.dynamic_index_in_dim(split, pos[2], 2, False)
    other = lax.dynamic_index_in_dim(split, 1 - pos[2], 2, False)
    ua = mine.transpose(1, 2, 0).reshape(D // 2, T)
    ub = shift(other.transpose(1, 2, 0).reshape(D // 2, T), dc=1)

    high, low, ua, ub = lax.optimization_barrier((high, low, ua, ub))
    row = jnp.concatenate([near, high, low], axis=0)
    up, down = shift(row, dy=1), shift(row, dy=-1)

    def with_id(rows, number):
        edge = jnp.broadcast_to(number.reshape(1, 1).astype(bf16), (16, PROJ))
        return jnp.concatenate([rows, edge], axis=0)

    far_a = shift(with_id(row[:256], ids[0, 0]), dx=1)
    far_b = shift(with_id(row[256:], ids[0, -1]), dx=-1)
    own = [row, up, down, far_a, far_b]
    pieces = own + [shift(piece[:512] if i < 3 else piece, dc=1) for i, piece in enumerate(own)]

    (w_abs, b, c, bb, cc, sig, stept, cumt, cum3, ew2, re2, cross2, vecs, s_end, g_in, link,
     linkn) = prep(pos, u, x, dyv, idc, a_log, dt_bias, d_skip, pieces)

    r1, b1 = from_seq(s_end, -1), from_seq(g_in, 1)
    y_in, dx_in, dyr, xw, d, row_in, col_in, ds, dbc, token = intra(
        x, dyv, cumt, stept, cum3, ew2, re2, cross2, b, c, bb, cc, idc, idr
    )
    m1, n1 = hop(r1, b1, vecs, token)
    r2, b2 = from_seq(m1, -1), from_seq(n1, 1)
    got = (r1, r2, b1, b2)
    shared = (vecs, bb, cc, link, linkn)
    dround, dlow = post(
        *got, dyr, xw, *shared, d, row_in, col_in, ds, dbc, sig, b, c, idc, idr, a_log
    )
    dother = shift(dround, dc=1)
    g0, g1, g3, g2a, g2b = gradw(pos, ua, ub, dround, dother)
    parts_y = (
        g0, shift(g1, dy=-1), shift(g3, dy=1), shift(g2a, dx=-1), shift(g2b, dx=1)
    )
    out_u, token = gradu(dround, dlow, w_abs)
    near, up, down = sums(sum_y_kernel, ((192, f32), (192, bf16), (128, bf16)), parts_y, token)
    up, down = shift(up, dz=-3), shift(down, dz=3)
    out_y, out_x, token = finish(*got, *shared, x, dyv, y_in, dx_in, ew2, re2, token)
    here, left, right = sums(
        sum_z_kernel, ((64, f32), (64, bf16), (64, bf16)), (near, up, down), token
    )
    part = here + shift(right, dz=-1).astype(f32) + shift(left, dz=1).astype(f32)
    grad_w = sum(
        fetch(part, lambda y, z, c, x, k=k: (y + 2 * ((x + k) % 2), z, c, x + k))
        for k in range(NX)
    )
    return out_y[None], out_x[None], out_u[None], grad_w


def solution(mesh):
    return jax.shard_map(
        body,
        mesh=mesh,
        in_specs=(
            P("dp", "seq", None), P("dp", "seq", None), P("dp", "seq"), P("dp", "seq", None),
            P("dp", None), P(), P(), P(),
        ),
        out_specs=(P("dp", "seq", None), P("dp", "seq", None), P("dp", "seq", None), P("dp", None)),
        check_vma=False,
    )
```

time: 651 us -> 196 us (0.30)
  waiting for transfers between devices: 451 us -> 60 us
  matrix products: 97.7 us -> 0 us
  Pallas kernels: 0 us -> 53.3 us
  starting transfers between devices: 24.2 us -> 58.2 us
  local copies, waits for them, and re-layouts: 35.1 us -> 15.7 us
  other arithmetic: 19 us -> 2.19 us
  between operations: 17.7 us -> 4.36 us
    ppermute x7 -> x32, waiting for transfers between devices: 233 us -> 60 us  [the longest x28 30.1 us: fetch(): return lax.ppermute(value, ('dp', 'seq'), pairs)]
    unnamed x4 -> x0, waiting for transfers between devices: 113 us -> none
    dot_general x15 -> x0, matrix products: 97.7 us -> none  [the longest x3 41.3 us: span_forward(): jnp.einsum('hts,shp->thp', mixing, xh, precision=lax.Precision.HIGHEST)]
    all_gather x1 -> x0, waiting for transfers between devices: 67.6 us -> none  [body(): weights = lax.all_gather(w_in, 'dp', axis=0, tiled=True)]
    pallas_call x0 -> x9, Pallas kernels: none -> 53.3 us  [the longest x1 20.2 us: intra(): pl.pallas_call(intra_kernel, grid=(H // GH,), out_shape=(shape(T, D), sha...]
    psum x1 -> x0, waiting for transfers between devices: 37.6 us -> none  [body(): summed = lax.psum(partial_w, 'seq')]
    ppermute x7 -> x32, starting transfers between devices: 24.1 us -> 58.2 us  [the longest x28 49.3 us: fetch(): return lax.ppermute(value, ('dp', 'seq'), pairs)]
    unnamed x50 -> x76, local copies, waits for them, and re-layouts: 28 us -> 10.3 us
  transfers between devices with their start and end apart: 10 -> 32, of which waited for: 9 -> 18; matrix products, arithmetic and copies ran while one was open for 13% -> 2% of each run, Pallas kernels for 0% -> 16%
where the time goes in v1:
time: 196 us; the launch traced here: 194 us
  waiting for transfers between devices  60 us (31%)
  starting transfers between devices  58.2 us (30%)
  Pallas kernels  53.3 us (27%)
  local copies, waits for them, and re-layouts  15.7 us (8%)
  between operations  4.36 us (2%)
  other arithmetic  2.19 us (1%)
    ppermute x28, starting transfers between devices, fetch(): return lax.ppermute(value, ('dp', 'seq'), pairs)  49.3 us
    ppermute x28, waiting for transfers between devices, fetch(): return lax.ppermute(value, ('dp', 'seq'), pairs)  30.1 us
    ppermute x4, waiting for transfers between devices, from_seq(): return lax.ppermute(value, 'seq', pairs)  30 us
    pallas_call x1, Pallas kernels, intra(): pl.pallas_call(intra_kernel, grid=(H // GH,), out_shape=(shape(T, D), sha...  20.2 us
    unnamed x76, local copies, waits for them, and re-layouts  10.3 us
    pallas_call x1, Pallas kernels, prep(): pl.pallas_call(prep_kernel, out_shape=(shape(D, PROJ, bf16), shape(T, N),...  10.2 us
    ppermute x4, starting transfers between devices, from_seq(): return lax.ppermute(value, 'seq', pairs)  8.92 us
    pallas_call x1, Pallas kernels, post(): pl.pallas_call(post_kernel, grid=(D // PL,), out_shape=(jax.ShapeDtypeStr...  8.24 us
  transfers between devices with their start and end apart: 32, of which 18 were waited for; matrix products, arithmetic and copies ran while one was open for 2% of the time, Pallas kernels for 16%

profile of v1, /device:TPU:8, one launch (start us, length us, event | category | flops | bytes accessed | tf_op | source)
XLA Modules:
  0.0 193.9 jit_solution(7491779433664622502)
XLA Ops:
  0.6 2.0 %collective-permute-start = (bf16[64,320]{1,0:T(8,128)(2,1)}, bf16[64,320]{1,0:T(8,128)(2,1)S(1)}, u32[]{:S(2)}, u32[]{:S(2)}) collective-permute-start(bf16[64,320]{1,0:T(8,128)(2,1)} %param.12), channel_id=1, source_target_pairs={{56,0},{185,1},{58,2},{187,3},{60,4},{189,5},{62,6},{191,7},{0,8},... | collective-permute-start | bytes 122888 | tf_op jit(solution)/shard_map/ppermute | solution.py:33
  2.6 4.0 %collective-permute-start.2 = (bf16[64,320]{1,0:T(8,128)(2,1)}, bf16[64,320]{1,0:T(8,128)(2,1)S(1)}, u32[]{:S(2)}, u32[]{:S(2)}) collective-permute-start(bf16[64,320]{1,0:T(8,128)(2,1)} %param.12), channel_id=1, source_target_pairs={{8,0},{137,1},{10,2},{139,3},{12,4},{141,5},{14,6},{143,7},{16,8},... | collective-permute-start | bytes 122888 | tf_op jit(solution)/shard_map/ppermute | solution.py:33
  6.7 1.4 collective-permute-start.1
  12.0 3.3 %copy.14 = bf16[256,4096]{0,1:T(8,128)(2,1)S(1)} copy(bf16[256,4096]{1,0:T(8,128)(2,1)} %bitcast.39) | data formatting | bytes 4194304 | tf_op jit(solution)/shard_map/optimization_barrier | solution.py:519
  16.7 5.2 %collective-permute-start.4 = (bf16[128,320]{1,0:T(8,128)(2,1)S(1)}, bf16[128,320]{1,0:T(8,128)(2,1)S(1)}, u32[]{:S(2)}, u32[]{:S(2)}) collective-permute-start(bf16[128,320]{1,0:T(8,128)(2,1)S(1)} %pad_maximum_fusion.4), channel_id=1, source_target_pairs={{40,0},{41,1},{42,2},{43,3},{44,4},{45,5},{46,6},{47,7},{48,8},{49... | collective-permute-start | bytes 245768 | tf_op jit(solution)/shard_map/ppermute | solution.py:33
  22.0 5.0 %collective-permute-done.4 = bf16[128,320]{1,0:T(8,128)(2,1)S(1)} collective-permute-done((bf16[128,320]{1,0:T(8,128)(2,1)S(1)}, bf16[128,320]{1,0:T(8,128)(2,1)S(1)}, u32[]{:S(2)}, u32[]{:S(2)}) %collective-permute-start.4) | collective-permute-done | bytes 81952 | tf_op jit(solution)/shard_map/ppermute | solution.py:33
  27.1 5.6 %collective-permute-done.3 = bf16[192,320]{1,0:T(8,128)(2,1)S(1)} collective-permute-done((bf16[192,320]{1,0:T(8,128)(2,1)S(1)}, bf16[192,320]{1,0:T(8,128)(2,1)S(1)}, u32[]{:S(2)}, u32[]{:S(2)}) %collective-permute-start.3) | collective-permute-done | bytes 122912 | tf_op jit(solution)/shard_map/ppermute | solution.py:33
  33.8 1.7 collective-permute-start.7
  37.9 7.3 %collective-permute-start.9 = (bf16[272,320]{1,0:T(8,128)(2,1)S(1)}, bf16[272,320]{1,0:T(8,128)(2,1)S(1)}, u32[]{:S(2)}, u32[]{:S(2)}) collective-permute-start(bf16[272,320]{1,0:T(8,128)(2,1)S(1)} %get-tuple-element.120), channel_id=1, source_target_pairs={{3,0},{0,1},{1,2},{2,3},{7,4},{4,5},{5,6},{6,7},{11,8},{8,9},{9,10... | collective-permute-start | bytes 522248 | tf_op jit(solution)/shard_map/ppermute | solution.py:33
  47.2 3.1 %collective-permute-done.9.refs_4_ = bf16[272,320]{1,0:T(8,128)(2,1)S(1)} collective-permute-done((bf16[272,320]{1,0:T(8,128)(2,1)S(1)}, bf16[272,320]{1,0:T(8,128)(2,1)S(1)}, u32[]{:S(2)}, u32[]{:S(2)}) %collective-permute-start.9) | collective-permute-done | bytes 174112 | tf_op jit(solution)/shard_map/ppermute | solution.py:33
  53.7 10.2 %shard_map.111 = (bf16[4096,320]{1,0:T(8,128)(2,1)}, f32[256,128]{1,0:T(8,128)}, f32[256,128]{1,0:T(8,128)}, bf16[256,256]{1,0:T(8,128)(2,1)}, bf16[256,256]{1,0...) custom-call(s32[4]{0:T(128)} %copy-done.25, ...), custom_call_target="tpu_custom_call" | custom-call | flops 1048576 | bytes 65536 | tf_op jit(solution)/shard_map/pallas_call | solution.py:165
  63.9 2.6 %collective-permute-start.15 = (bf16[128,4096]{1,0:T(8,128)(2,1)}, bf16[128,4096]{1,0:T(8,128)(2,1)S(1)}, u32[]{:S(2)}, u32[]{:S(2)}) collective-permute-start(bf16[128,4096]{1,0:T(8,128)(2,1)} %get-tuple-element.69), channel_id=1, source_target_pairs={{0,1},{1,2},{2,3},{4,5},{5,6},{6,7},{8,9},{9,10},{10,11},{12,13},{... | collective-permute-start | bytes 3145736 | tf_op jit(solution)/shard_map/ppermute | solution.py:42
  67.9 20.2 %shard_map.112 = (f32[256,4096]{1,0:T(8,128)}, f32[256,4096]{1,0:T(8,128)}, bf16[256,4096]{1,0:T(8,128)(2,1)}, bf16[256,4096]{1,0:T(8,128)(2,1)}, f32[256,64]{1,...) custom-call(bf16[256,4096]{1,0:T(8,128)(2,1)} %bitcast.29, ...), custom_call_target="tpu_custom_call" | custom-call | flops 1048576 | bytes 65536 | tf_op jit(solution)/shard_map/pallas_call | solution.py:275
  89.5 4.3 %collective-permute-done.16.back.b1 = bf16[128,4096]{1,0:T(8,128)(2,1)S(1)} collective-permute-done((bf16[128,4096]{1,0:T(8,128)(2,1)}, bf16[128,4096]{1,0:T(8,128)(2,1)S(1)}, u32[]{:S(2)}, u32[]{:S(2)}) %collective-permute-start.16) | collective-permute-done | bytes 1048608 | tf_op jit(solution)/shard_map/ppermute | solution.py:42
  95.2 3.7 %collective-permute-start.17 = (bf16[128,4096]{1,0:T(8,128)(2,1)S(1)}, bf16[128,4096]{1,0:T(8,128)(2,1)S(1)}, u32[]{:S(2)}, u32[]{:S(2)}) collective-permute-start(bf16[128,4096]{1,0:T(8,128)(2,1)S(1)} %get-tuple-element.83), channel_id=1, source_target_pairs={{0,1},{1,2},{2,3},{4,5},{5,6},{6,7},{8,9},{9,10},{10,11},{12,13},{... | collective-permute-start | bytes 3145736 | tf_op jit(solution)/shard_map/ppermute | solution.py:42
  100.2 20.2 %collective-permute-done.17.r2 = bf16[128,4096]{1,0:T(8,128)(2,1)S(1)} collective-permute-done((bf16[128,4096]{1,0:T(8,128)(2,1)S(1)}, bf16[128,4096]{1,0:T(8,128)(2,1)S(1)}, u32[]{:S(2)}, u32[]{:S(2)}) %collective-permute-start.17) | collective-permute-done | bytes 1048608 | tf_op jit(solution)/shard_map/ppermute | solution.py:42
  120.4 4.2 %collective-permute-done.18.b2 = bf16[128,4096]{1,0:T(8,128)(2,1)S(1)} collective-permute-done((bf16[128,4096]{1,0:T(8,128)(2,1)S(1)}, bf16[128,4096]{1,0:T(8,128)(2,1)S(1)}, u32[]{:S(2)}, u32[]{:S(2)}) %collective-permute-start.18) | collective-permute-done | bytes 1048608 | tf_op jit(solution)/shard_map/ppermute | solution.py:42
  124.7 1.6 copy-done.7
  130.8 8.2 %shard_map.114 = (bf16[256,320]{1,0:T(8,128)(2,1)S(1)}, bf16[256,320]{1,0:T(8,128)(2,1)S(1)}) custom-call(bf16[128,4096]{1,0:T(8,128)(2,1)S(1)} %collective-permute-done.15.one.r1, bf16[128,4096]{1,0:T(8,128)(2,1)S(1)} %collective-permute-done.17.r2, bf16[128,4096]{1,0:T(8,128)(2,1)S(1)} %collective-permute-done.16.back.b1, ...), custom_call_target="tpu_custom_call" | custom-call | flops 1048576 | bytes 65536 | tf_op jit(solution)/shard_map/pallas_call | solution.py:392
  139.3 1.4 collective-permute-done.19.db
  142.0 2.7 %shard_map.117 = (f32[512,320]{1,0:T(8,128)S(1)}, bf16[512,320]{1,0:T(8,128)(2,1)S(1)}, bf16[512,320]{1,0:T(8,128)(2,1)S(1)}, bf16[256,320]{1,0:T(8,128)(2,1)S(1)}, bf16[256,320]{1,0:T(8,128)(2,1)S(1)}) custom-call(s32[4]{0:T(128)S(1)} %copy-done.26, bf16[2048,256]{1,0:T(8,128)(2,1)S(1)} %bitcast.34, bf16[2048,256]{1,0:T(8,128)(2,1)S(1)} %copy-done.12, ...), custom_call_target="tpu_custom_call" | custom-call | flops 1048576 | bytes 65536 | tf_op jit(solution)/shard_map/pallas_call | solution.py:425
  144.8 3.3 %collective-permute-start.21 = (bf16[512,320]{1,0:T(8,128)(2,1)S(1)}, bf16[512,320]{1,0:T(8,128)(2,1)S(1)}, u32[]{:S(2)}, u32[]{:S(2)}) collective-permute-start(bf16[512,320]{1,0:T(8,128)(2,1)S(1)} %get-tuple-element.108), channel_id=1, source_target_pairs={{64,0},{65,1},{66,2},{67,3},{68,4},{69,5},{70,6},{71,7},{72,8},{73... | collective-permute-start | bytes 983048 | tf_op jit(solution)/shard_map/ppermute | solution.py:33
  149.2 2.0 %collective-permute-start.23 = (bf16[256,320]{1,0:T(8,128)(2,1)S(1)}, bf16[256,320]{1,0:T(8,128)(2,1)S(1)}, u32[]{:S(2)}, u32[]{:S(2)}) collective-permute-start(bf16[256,320]{1,0:T(8,128)(2,1)S(1)} %get-tuple-element.110), channel_id=1, source_target_pairs={{1,0},{2,1},{3,2},{0,3},{5,4},{6,5},{7,6},{4,7},{9,8},{10,9},{11,1... | collective-permute-start | bytes 491528 | tf_op jit(solution)/shard_map/ppermute | solution.py:33
  151.3 3.8 %shard_map.115 = (bf16[256,4096]{1,0:T(8,128)(2,1)}, f32[8,128]{1,0:T(8,128)S(1)}) custom-call(bf16[256,320]{1,0:T(8,128)(2,1)S(1)} %get-tuple-element.97.dhi.da, bf16[256,320]{1,0:T(8,128)(2,1)S(1)} %get-tuple-element.98.dlo, bf16[4096,320]{1,0:T(8,128)(2,1)S(1)} %copy-done.4), custom_call_target="tpu_custom_call" | custom-call | flops 1048576 | bytes 65536 | tf_op jit(solution)/shard_map/pallas_call | solution.py:442
  155.9 1.4 collective-permute-done.20.up
  157.5 6.7 %collective-permute-start.24 = (bf16[192,320]{1,0:T(8,128)(2,1)S(1)}, bf16[192,320]{1,0:T(8,128)(2,1)S(1)}, u32[]{:S(2)}, u32[]{:S(2)}) collective-permute-start(bf16[192,320]{1,0:T(8,128)(2,1)S(1)} %get-tuple-element.112), channel_id=1, source_target_pairs={{40,0},{41,1},{42,2},{43,3},{44,4},{45,5},{46,6},{47,7},{48,8},{49... | collective-permute-start | bytes 368648 | tf_op jit(solution)/shard_map/ppermute | solution.py:33
  164.2 7.2 %shard_map.116 = (bf16[256,4096]{1,0:T(8,128)(2,1)}, bf16[256,4096]{1,0:T(8,128)(2,1)}, f32[8,128]{1,0:T(8,128)S(1)}) custom-call(bf16[128,4096]{1,0:T(8,128)(2,1)S(1)} %collective-permute-done.15.one.r1, bf16[128,4096]{1,0:T(8,128)(2,1)S(1)} %collective-permute-done.17.r2, bf16[128,4096]{1,0:T(8,128)(2,1)S(1)} %collective-permute-done.16.back.b1, ...), custom_call_target="tpu_custom_call" | custom-call | flops 1048576 | bytes 65536 | tf_op jit(solution)/shard_map/pallas_call | solution.py:468
  171.4 2.0 %collective-permute-done.25.down = bf16[128,320]{1,0:T(8,128)(2,1)S(1)} collective-permute-done((bf16[128,320]{1,0:T(8,128)(2,1)S(1)}, bf16[128,320]{1,0:T(8,128)(2,1)S(1)}, u32[]{:S(2)}, u32[]{:S(2)}) %collective-permute-start.25) | collective-permute-done | bytes 81952 | tf_op jit(solution)/shard_map/ppermute | solution.py:33
  173.5 1.9 collective-permute-start.26
  176.8 2.1 %collective-permute-done.26 = bf16[64,320]{1,0:T(8,128)(2,1)S(1)} collective-permute-done((bf16[64,320]{1,0:T(8,128)(2,1)S(1)}, bf16[64,320]{1,0:T(8,128)(2,1)S(1)}, u32[]{:S(2)}, u32[]{:S(2)}) %collective-permute-start.26) | collective-permute-done | bytes 40992 | tf_op jit(solution)/shard_map/ppermute | solution.py:33
  181.9 5.2 %collective-permute-start.29 = (f32[64,320]{1,0:T(8,128)S(1)}, f32[64,320]{1,0:T(8,128)S(1)}, u32[]{:S(2)}, u32[]{:S(2)}) collective-permute-start(f32[64,320]{1,0:T(8,128)S(1)} %convert_add_fusion), channel_id=1, source_target_pairs={{129,0},{2,1},{131,2},{0,3},{133,4},{6,5},{135,6},{4,7},{137,8},{1... | collective-permute-start | bytes 245768 | tf_op jit(solution)/shard_map/ppermute | solution.py:33
  187.8 5.4 %collective-permute-done.29 = f32[64,320]{1,0:T(8,128)S(1)} collective-permute-done((f32[64,320]{1,0:T(8,128)S(1)}, f32[64,320]{1,0:T(8,128)S(1)}, u32[]{:S(2)}, u32[]{:S(2)}) %collective-permute-start.29) | collective-permute-done | bytes 81952 | tf_op jit(solution)/shard_map/ppermute | solution.py:33
  (130 shorter events, 30.5 us)
Async XLA Ops:
  0.6 8.2 %collective-permute-start = (bf16[64,320]{1,0:T(8,128)(2,1)}, bf16[64,320]{1,0:T(8,128)(2,1)S(1)}, u32[]{:S(2)}, u32[]{:S(2)}) collective-permute-start(bf16[64,320]{1,0:T(8,128)(2,1)} %param.12), channel_id=1, source_target_pairs={{56,0},{185,1},{58,2},{187,3},{60,4},{189,5},{62,6},{191,7},{0,8},... | collective-permute-start | bytes 122888 | tf_op jit(solution)/shard_map/ppermute | solution.py:33
  2.6 6.2 %collective-permute-start.2 = (bf16[64,320]{1,0:T(8,128)(2,1)}, bf16[64,320]{1,0:T(8,128)(2,1)S(1)}, u32[]{:S(2)}, u32[]{:S(2)}) collective-permute-start(bf16[64,320]{1,0:T(8,128)(2,1)} %param.12), channel_id=1, source_target_pairs={{8,0},{137,1},{10,2},{139,3},{12,4},{141,5},{14,6},{143,7},{16,8},... | collective-permute-start | bytes 122888 | tf_op jit(solution)/shard_map/ppermute | solution.py:33
  6.7 2.2 %collective-permute-start.1 = (bf16[64,320]{1,0:T(8,128)(2,1)}, bf16[64,320]{1,0:T(8,128)(2,1)S(1)}, u32[]{:S(2)}, u32[]{:S(2)}) collective-permute-start(bf16[64,320]{1,0:T(8,128)(2,1)} %param.12), channel_id=1, source_target_pairs={{0,0},{129,1},{2,2},{131,3},{4,4},{133,5},{6,6},{135,7},{8,8},{137... | collective-permute-start | bytes 122888 | tf_op jit(solution)/shard_map/ppermute | solution.py:33
  16.2 16.5 %collective-permute-start.5 = (bf16[2048,256]{1,0:T(8,128)(2,1)S(1)}, bf16[2048,256]{1,0:T(8,128)(2,1)S(1)}, u32[]{:S(2)}, u32[]{:S(2)}) collective-permute-start(bf16[2048,256]{1,0:T(8,128)(2,1)S(1)} %bitcast.41), channel_id=1, source_target_pairs={{4,0},{5,1},{6,2},{7,3},{0,4},{1,5},{2,6},{3,7},{12,8},{13,9},{14,... | collective-permute-start | bytes 3145736 | tf_op jit(solution)/shard_map/ppermute | solution.py:33
  16.7 10.4 %collective-permute-start.4 = (bf16[128,320]{1,0:T(8,128)(2,1)S(1)}, bf16[128,320]{1,0:T(8,128)(2,1)S(1)}, u32[]{:S(2)}, u32[]{:S(2)}) collective-permute-start(bf16[128,320]{1,0:T(8,128)(2,1)S(1)} %pad_maximum_fusion.4), channel_id=1, source_target_pairs={{40,0},{41,1},{42,2},{43,3},{44,4},{45,5},{46,6},{47,7},{48,8},{49... | collective-permute-start | bytes 245768 | tf_op jit(solution)/shard_map/ppermute | solution.py:33
  21.9 10.8 %collective-permute-start.3 = (bf16[192,320]{1,0:T(8,128)(2,1)S(1)}, bf16[192,320]{1,0:T(8,128)(2,1)S(1)}, u32[]{:S(2)}, u32[]{:S(2)}) collective-permute-start(bf16[192,320]{1,0:T(8,128)(2,1)S(1)} %pad_maximum_fusion.3), channel_id=1, source_target_pairs={{24,0},{25,1},{26,2},{27,3},{28,4},{29,5},{30,6},{31,7},{32,8},{33... | collective-permute-start | bytes 368648 | tf_op jit(solution)/shard_map/ppermute | solution.py:33
  33.8 12.8 %collective-permute-start.7 = (bf16[512,320]{1,0:T(8,128)(2,1)S(1)}, bf16[512,320]{1,0:T(8,128)(2,1)S(1)}, u32[]{:S(2)}, u32[]{:S(2)}) collective-permute-start(bf16[512,320]{1,0:T(8,128)(2,1)S(1)} %constant_dynamic-update-slice_fusion.refs_0_), channel_id=1, source_target_pairs={{192,0},{193,1},{194,2},{195,3},{196,4},{197,5},{198,6},{199,7},{2... | collective-permute-start | bytes 983048 | tf_op jit(solution)/shard_map/ppermute | solution.py:33
  35.5 11.6 %collective-permute-start.6 = (bf16[512,320]{1,0:T(8,128)(2,1)S(1)}, bf16[512,320]{1,0:T(8,128)(2,1)S(1)}, u32[]{:S(2)}, u32[]{:S(2)}) collective-permute-start(bf16[512,320]{1,0:T(8,128)(2,1)S(1)} %constant_dynamic-update-slice_fusion.refs_0_), channel_id=1, source_target_pairs={{64,0},{65,1},{66,2},{67,3},{68,4},{69,5},{70,6},{71,7},{72,8},{73... | collective-permute-start | bytes 983048 | tf_op jit(solution)/shard_map/ppermute | solution.py:33
  37.9 12.3 %collective-permute-start.9 = (bf16[272,320]{1,0:T(8,128)(2,1)S(1)}, bf16[272,320]{1,0:T(8,128)(2,1)S(1)}, u32[]{:S(2)}, u32[]{:S(2)}) collective-permute-start(bf16[272,320]{1,0:T(8,128)(2,1)S(1)} %get-tuple-element.120), channel_id=1, source_target_pairs={{3,0},{0,1},{1,2},{2,3},{7,4},{4,5},{5,6},{6,7},{11,8},{8,9},{9,10... | collective-permute-start | bytes 522248 | tf_op jit(solution)/shard_map/ppermute | solution.py:33
  45.2 5.9 %collective-permute-start.8 = (bf16[272,320]{1,0:T(8,128)(2,1)S(1)}, bf16[272,320]{1,0:T(8,128)(2,1)}, u32[]{:S(2)}, u32[]{:S(2)}) collective-permute-start(bf16[272,320]{1,0:T(8,128)(2,1)S(1)} %get-tuple-element.121), channel_id=1, source_target_pairs={{1,0},{2,1},{3,2},{0,3},{5,4},{6,5},{7,6},{4,7},{9,8},{10,9},{11,1... | collective-permute-start | bytes 522248 | tf_op jit(solution)/shard_map/ppermute | solution.py:33
  46.6 5.4 %collective-permute-start.10 = (bf16[512,320]{1,0:T(8,128)(2,1)S(1)}, bf16[512,320]{1,0:T(8,128)(2,1)S(1)}, u32[]{:S(2)}, u32[]{:S(2)}) collective-permute-start(bf16[512,320]{1,0:T(8,128)(2,1)S(1)} %constant_dynamic-update-slice_fusion.refs_0_), channel_id=1, source_target_pairs={{4,0},{5,1},{6,2},{7,3},{0,4},{1,5},{2,6},{3,7},{12,8},{13,9},{14,... | collective-permute-start | bytes 983048 | tf_op jit(solution)/shard_map/ppermute | solution.py:33
  46.6 6.3 %collective-permute-start.12 = (bf16[512,320]{1,0:T(8,128)(2,1)S(1)}, bf16[512,320]{1,0:T(8,128)(2,1)S(1)}, u32[]{:S(2)}, u32[]{:S(2)}) collective-permute-start(bf16[512,320]{1,0:T(8,128)(2,1)S(1)} %collective-permute-done.7.refs_2_), channel_id=1, source_target_pairs={{4,0},{5,1},{6,2},{7,3},{0,4},{1,5},{2,6},{3,7},{12,8},{13,9},{14,... | collective-permute-start | bytes 983048 | tf_op jit(solution)/shard_map/ppermute | solution.py:33
  47.1 5.8 %collective-permute-start.11 = (bf16[512,320]{1,0:T(8,128)(2,1)S(1)}, bf16[512,320]{1,0:T(8,128)(2,1)}, u32[]{:S(2)}, u32[]{:S(2)}) collective-permute-start(bf16[512,320]{1,0:T(8,128)(2,1)S(1)} %collective-permute-done.6.refs_1_), channel_id=1, source_target_pairs={{4,0},{5,1},{6,2},{7,3},{0,4},{1,5},{2,6},{3,7},{12,8},{13,9},{14,... | collective-permute-start | bytes 983048 | tf_op jit(solution)/shard_map/ppermute | solution.py:33
  50.3 1.7 collective-permute-start.14
  51.1 1.8 collective-permute-start.13
  63.9 25.6 %collective-permute-start.15 = (bf16[128,4096]{1,0:T(8,128)(2,1)}, bf16[128,4096]{1,0:T(8,128)(2,1)S(1)}, u32[]{:S(2)}, u32[]{:S(2)}) collective-permute-start(bf16[128,4096]{1,0:T(8,128)(2,1)} %get-tuple-element.69), channel_id=1, source_target_pairs={{0,1},{1,2},{2,3},{4,5},{5,6},{6,7},{8,9},{9,10},{10,11},{12,13},{... | collective-permute-start | bytes 3145736 | tf_op jit(solution)/shard_map/ppermute | solution.py:42
  66.6 27.3 %collective-permute-start.16 = (bf16[128,4096]{1,0:T(8,128)(2,1)}, bf16[128,4096]{1,0:T(8,128)(2,1)S(1)}, u32[]{:S(2)}, u32[]{:S(2)}) collective-permute-start(bf16[128,4096]{1,0:T(8,128)(2,1)} %get-tuple-element.70), channel_id=1, source_target_pairs={{1,0},{2,1},{3,2},{5,4},{6,5},{7,6},{9,8},{10,9},{11,10},{13,12},{... | collective-permute-start | bytes 3145736 | tf_op jit(solution)/shard_map/ppermute | solution.py:42
  95.2 25.2 %collective-permute-start.17 = (bf16[128,4096]{1,0:T(8,128)(2,1)S(1)}, bf16[128,4096]{1,0:T(8,128)(2,1)S(1)}, u32[]{:S(2)}, u32[]{:S(2)}) collective-permute-start(bf16[128,4096]{1,0:T(8,128)(2,1)S(1)} %get-tuple-element.83), channel_id=1, source_target_pairs={{0,1},{1,2},{2,3},{4,5},{5,6},{6,7},{8,9},{9,10},{10,11},{12,13},{... | collective-permute-start | bytes 3145736 | tf_op jit(solution)/shard_map/ppermute | solution.py:42
  98.9 25.7 %collective-permute-start.18 = (bf16[128,4096]{1,0:T(8,128)(2,1)S(1)}, bf16[128,4096]{1,0:T(8,128)(2,1)S(1)}, u32[]{:S(2)}, u32[]{:S(2)}) collective-permute-start(bf16[128,4096]{1,0:T(8,128)(2,1)S(1)} %get-tuple-element.84), channel_id=1, source_target_pairs={{1,0},{2,1},{3,2},{5,4},{6,5},{7,6},{9,8},{10,9},{11,10},{13,12},{... | collective-permute-start | bytes 3145736 | tf_op jit(solution)/shard_map/ppermute | solution.py:42
  139.0 1.7 collective-permute-start.19
  144.7 12.7 %collective-permute-start.20 = (bf16[512,320]{1,0:T(8,128)(2,1)S(1)}, bf16[512,320]{1,0:T(8,128)(2,1)S(1)}, u32[]{:S(2)}, u32[]{:S(2)}) collective-permute-start(bf16[512,320]{1,0:T(8,128)(2,1)S(1)} %get-tuple-element.107), channel_id=1, source_target_pairs={{192,0},{193,1},{194,2},{195,3},{196,4},{197,5},{198,6},{199,7},{2... | collective-permute-start | bytes 983048 | tf_op jit(solution)/shard_map/ppermute | solution.py:33
  144.8 12.6 %collective-permute-start.21 = (bf16[512,320]{1,0:T(8,128)(2,1)S(1)}, bf16[512,320]{1,0:T(8,128)(2,1)S(1)}, u32[]{:S(2)}, u32[]{:S(2)}) collective-permute-start(bf16[512,320]{1,0:T(8,128)(2,1)S(1)} %get-tuple-element.108), channel_id=1, source_target_pairs={{64,0},{65,1},{66,2},{67,3},{68,4},{69,5},{70,6},{71,7},{72,8},{73... | collective-permute-start | bytes 983048 | tf_op jit(solution)/shard_map/ppermute | solution.py:33
  148.0 7.9 %collective-permute-start.22 = (bf16[256,320]{1,0:T(8,128)(2,1)S(1)}, bf16[256,320]{1,0:T(8,128)(2,1)S(1)}, u32[]{:S(2)}, u32[]{:S(2)}) collective-permute-start(bf16[256,320]{1,0:T(8,128)(2,1)S(1)} %get-tuple-element.109), channel_id=1, source_target_pairs={{3,0},{0,1},{1,2},{2,3},{7,4},{4,5},{5,6},{6,7},{11,8},{8,9},{9,10... | collective-permute-start | bytes 491528 | tf_op jit(solution)/shard_map/ppermute | solution.py:33
  149.2 6.7 %collective-permute-start.23 = (bf16[256,320]{1,0:T(8,128)(2,1)S(1)}, bf16[256,320]{1,0:T(8,128)(2,1)S(1)}, u32[]{:S(2)}, u32[]{:S(2)}) collective-permute-start(bf16[256,320]{1,0:T(8,128)(2,1)S(1)} %get-tuple-element.110), channel_id=1, source_target_pairs={{1,0},{2,1},{3,2},{0,3},{5,4},{6,5},{7,6},{4,7},{9,8},{10,9},{11,1... | collective-permute-start | bytes 491528 | tf_op jit(solution)/shard_map/ppermute | solution.py:33
  157.5 15.9 %collective-permute-start.24 = (bf16[192,320]{1,0:T(8,128)(2,1)S(1)}, bf16[192,320]{1,0:T(8,128)(2,1)S(1)}, u32[]{:S(2)}, u32[]{:S(2)}) collective-permute-start(bf16[192,320]{1,0:T(8,128)(2,1)S(1)} %get-tuple-element.112), channel_id=1, source_target_pairs={{40,0},{41,1},{42,2},{43,3},{44,4},{45,5},{46,6},{47,7},{48,8},{49... | collective-permute-start | bytes 368648 | tf_op jit(solution)/shard_map/ppermute | solution.py:33
  164.2 9.3 %collective-permute-start.25 = (bf16[128,320]{1,0:T(8,128)(2,1)S(1)}, bf16[128,320]{1,0:T(8,128)(2,1)S(1)}, u32[]{:S(2)}, u32[]{:S(2)}) collective-permute-start(bf16[128,320]{1,0:T(8,128)(2,1)S(1)} %get-tuple-element.113), channel_id=1, source_target_pairs={{24,0},{25,1},{26,2},{27,3},{28,4},{29,5},{30,6},{31,7},{32,8},{33... | collective-permute-start | bytes 245768 | tf_op jit(solution)/shard_map/ppermute | solution.py:33
  173.5 5.4 %collective-permute-start.26 = (bf16[64,320]{1,0:T(8,128)(2,1)S(1)}, bf16[64,320]{1,0:T(8,128)(2,1)S(1)}, u32[]{:S(2)}, u32[]{:S(2)}) collective-permute-start(bf16[64,320]{1,0:T(8,128)(2,1)S(1)} %get-tuple-element.116), channel_id=1, source_target_pairs={{56,0},{57,1},{58,2},{59,3},{60,4},{61,5},{62,6},{63,7},{0,8},{1,9... | collective-permute-start | bytes 122888 | tf_op jit(solution)/shard_map/ppermute | solution.py:33
  175.4 4.1 %collective-permute-start.27 = (bf16[64,320]{1,0:T(8,128)(2,1)S(1)}, bf16[64,320]{1,0:T(8,128)(2,1)S(1)}, u32[]{:S(2)}, u32[]{:S(2)}) collective-permute-start(bf16[64,320]{1,0:T(8,128)(2,1)S(1)} %get-tuple-element.117), channel_id=1, source_target_pairs={{8,0},{9,1},{10,2},{11,3},{12,4},{13,5},{14,6},{15,7},{16,8},{17,9... | collective-permute-start | bytes 122888 | tf_op jit(solution)/shard_map/ppermute | solution.py:33
  179.5 8.3 %collective-permute-start.31 = (f32[64,320]{1,0:T(8,128)S(1)}, f32[64,320]{1,0:T(8,128)S(1)}, u32[]{:S(2)}, u32[]{:S(2)}) collective-permute-start(f32[64,320]{1,0:T(8,128)S(1)} %convert_add_fusion), channel_id=1, source_target_pairs={{131,0},{0,1},{129,2},{2,3},{135,4},{4,5},{133,6},{6,7},{139,8},{8... | collective-permute-start | bytes 245768 | tf_op jit(solution)/shard_map/ppermute | solution.py:33
  180.8 7.0 %collective-permute-start.30 = (f32[64,320]{1,0:T(8,128)S(1)}, f32[64,320]{1,0:T(8,128)S(1)}, u32[]{:S(2)}, u32[]{:S(2)}) collective-permute-start(f32[64,320]{1,0:T(8,128)S(1)} %convert_add_fusion), channel_id=1, source_target_pairs={{2,0},{131,1},{0,2},{129,3},{6,4},{135,5},{4,6},{133,7},{10,8},{13... | collective-permute-start | bytes 245768 | tf_op jit(solution)/shard_map/ppermute | solution.py:33
  181.9 11.3 %collective-permute-start.29 = (f32[64,320]{1,0:T(8,128)S(1)}, f32[64,320]{1,0:T(8,128)S(1)}, u32[]{:S(2)}, u32[]{:S(2)}) collective-permute-start(f32[64,320]{1,0:T(8,128)S(1)} %convert_add_fusion), channel_id=1, source_target_pairs={{129,0},{2,1},{131,2},{0,3},{133,4},{6,5},{135,6},{4,7},{137,8},{1... | collective-permute-start | bytes 245768 | tf_op jit(solution)/shard_map/ppermute | solution.py:33
  187.1 6.1 %collective-permute-start.28 = (f32[64,320]{1,0:T(8,128)S(1)}, f32[64,320]{1,0:T(8,128)S(1)}, u32[]{:S(2)}, u32[]{:S(2)}) collective-permute-start(f32[64,320]{1,0:T(8,128)S(1)} %convert_add_fusion), channel_id=1, source_target_pairs={{0,0},{129,1},{2,2},{131,3},{4,4},{133,5},{6,6},{135,7},{8,8},{137... | collective-permute-start | bytes 245768 | tf_op jit(solution)/shard_map/ppermute | solution.py:33
  (36 other events, 734.2 us)
